TPU v7x, 256 devices: a whole 4x4x8 slice. The times are simulated.
256 devices in a mesh: dom: 32 (over x_lo, z, core), col: 8 (over x_hi, y).
Axes of the slice: x: 4 (x_hi: 2, x_lo: 2; x = x_hi * 2 + x_lo), y: 4, z: 8, core: 2. Of those that a mesh axis runs over, the one named last changes fastest.
Arguments:
- feats: bfloat16 [16384, 256], P('dom', 'col'), may hold values from -6 to 6
- w_first: bfloat16 [256, 256], replicated, may hold values from -0.375 to 0.375
- w_second: bfloat16 [256, 256], replicated, may hold values from -0.375 to 0.375
- block_cols: int32 [128, 32], P('dom'), may hold values from 0 to 127, as said below
- block_count: int32 [128], P('dom'), may hold values from 1 to 32
- block_vals: bfloat16 [128, 32, 128, 128], P('dom', 'col'), may hold values from -0.125 to 0.125
- cotangent: bfloat16 [16384, 256], P('dom', 'col'), may hold values from -6 to 6
Outputs:
- output: float32 [16384, 256], P('dom', 'col')
- grad_first: float32 [256, 256], P(None, 'col')
- grad_second: float32 [256, 256], P(None, 'col')
Inputs may be any that keep to these rules, and one draw needn't show every extreme that they name: Each row of block_cols names 32 different column blocks.
All inputs are finite; a program needn't handle non-finite values.
Results may differ from a plain program's by a relative error of at most 0.019.
Values may be sent and summed in bfloat16 or wider, within the bound.
A program may use at most 64 MiB of HBM per device.

v0:
```python
import jax
import jax.numpy as jnp
from jax import lax
from jax.sharding import Mesh
from jax.sharding import PartitionSpec as P

BLK = 128
DOM = ("dom_0", "dom_1", "dom_2")


def in_blocks(shard, dim, peers):
    before, after = (shard.shape[:dim], shard.shape[dim + 1 :])
    return jnp.moveaxis(shard.reshape(*before, peers, -1, *after), dim, 0)


def sum_by_chip(shard, chips, core, dim):
    sizes = (lax.axis_size(chips), lax.axis_size(core))
    pieces = in_blocks(shard, dim, sizes[0] * sizes[1])
    inside = pieces.shape[1:]
    pieces = pieces.reshape(*sizes, *inside).swapaxes(0, 1).reshape(-1, *inside)
    pieces = lax.psum_scatter(pieces, core, scatter_dimension=0, tiled=True)
    return lax.psum_scatter(pieces, chips, scatter_dimension=0, tiled=True)[0]


def joined_along(pieces, dim):
    shape = list(pieces.shape[1:])
    shape[dim] *= pieces.shape[0]
    return jnp.moveaxis(pieces, 0, dim).reshape(shape)


def sent_to_all(shard, axis):
    peers = lax.axis_size(axis)
    return lax.all_to_all(
        jnp.broadcast_to(shard[None], (peers, *shard.shape)), axis, 0, 0, tiled=True
    )


def gathered_copies(shard, axis, dim):
    return joined_along(sent_to_all(shard, axis), dim)


def over_copies(shard, axis):
    everything = sent_to_all(shard, axis)
    return jnp.sum(everything.astype(jnp.float32), axis=0)


def summed_on_arrival(shard, axis, dim):
    pieces = in_blocks(shard, dim, lax.axis_size(axis))
    arrived = lax.all_to_all(pieces, axis, split_axis=0, concat_axis=0, tiled=True)
    return arrived.sum(axis=0)


def silu_slope(value):
    sig = jax.nn.sigmoid(value)
    return sig + value * sig * (1.0 - sig)


def forward_fold(prod, cols, vals):
    rows, width = prod.shape
    piece = lax.all_gather(prod, DOM, axis=0, tiled=True)
    count_blocks = piece.shape[0] // BLK
    hit = (cols >= 0) & (cols < count_blocks)
    picked = piece.reshape(count_blocks, BLK, width)[jnp.clip(cols, 0, count_blocks - 1)]
    picked = jnp.where(hit[:, :, None, None], picked, jnp.zeros((), picked.dtype))
    contrib = jnp.einsum("rkij,rkjf->rif", vals, picked, preferred_element_type=jnp.float32)
    return contrib.reshape(rows, width)


def backward_scatter(grad, cols, vals):
    rows, width = grad.shape
    nblocks = rows // BLK
    products = jnp.einsum(
        "rkij,rif->rkjf",
        vals,
        grad.reshape(nblocks, BLK, width),
        preferred_element_type=jnp.float32,
    )
    count = rows * lax.axis_size(("dom_0", "dom_1")) * lax.axis_size("dom_2")
    count_blocks = count // BLK
    onehot = (cols[:, :, None] == jnp.arange(count_blocks)[None, None, :]).astype(jnp.float32)
    summed = jnp.einsum("rkp,rkjf->pjf", onehot, products, precision=lax.Precision.HIGHEST)
    return sum_by_chip(summed.reshape(count, width), ("dom_0", "dom_1"), "dom_2", 0)


def body(feats, w_first, w_second, block_cols, block_count, block_vals, cotangent):
    col_index = lax.axis_index("col")
    rows, narrow = feats.shape

    def widen(value):
        return gathered_copies(value, "col", 1)

    def weight_grad(full, back):
        return over_copies(
            jnp.dot(full.T, back, preferred_element_type=jnp.float32).astype(jnp.bfloat16), DOM
        ).astype(jnp.float32)

    all_vals = lax.all_gather(block_vals, "col", axis=1, tiled=True)
    slot_ids = jnp.arange(all_vals.shape[1])
    usable = slot_ids[None, :] < block_count[:, None]
    vals = jnp.where(usable[:, :, None, None], all_vals, jnp.zeros((), all_vals.dtype))

    def project(full, weight):
        weight_cols = lax.dynamic_slice_in_dim(weight, col_index * narrow, narrow, 1)
        return jnp.dot(full, weight_cols, preferred_element_type=jnp.float32).astype(jnp.bfloat16)

    def aggregate(prod):
        return forward_fold(prod, block_cols, vals)

    def transpose(grad):
        return backward_scatter(grad, block_cols, vals)

    full_input = widen(feats)
    first = aggregate(project(full_input, w_first))
    hidden = (first * jax.nn.sigmoid(first)).astype(jnp.bfloat16)
    full_hidden = widen(hidden)
    output = aggregate(project(full_hidden, w_second))
    back_second = transpose(cotangent).astype(jnp.bfloat16)
    grad_second = weight_grad(full_hidden, back_second)
    second_cols = lax.dynamic_slice_in_dim(w_second, col_index * narrow, narrow, 1)
    partial_hidden = jnp.dot(back_second, second_cols.T, preferred_element_type=jnp.float32)
    hidden_grad = summed_on_arrival(partial_hidden, "col", 1)
    act_grad = (hidden_grad * silu_slope(first)).astype(jnp.bfloat16)
    back_first = transpose(act_grad).astype(jnp.bfloat16)
    grad_first = weight_grad(full_input, back_first)
    return (output, grad_first, grad_second)


def solution(mesh):
    split = Mesh(
        mesh.devices.reshape(2, 8, 2, mesh.shape["col"]), ("dom_0", "dom_1", "dom_2", "col")
    )
    return jax.shard_map(
        body,
        mesh=split,
        in_specs=(
            P(DOM, "col"),
            P(),
            P(),
            P(DOM, None),
            P(DOM),
            P(DOM, "col", None, None),
            P(DOM, "col"),
        ),
        out_specs=(P(DOM, "col"), P(None, "col"), P(None, "col")),
        check_vma=False,
    )
```

profile of v0, /device:TPU:16, one launch (start us, length us, event | category | flops | bytes accessed | tf_op | source)
XLA Modules:
  0.0 338.7 jit_solution(4655881142837038771)
XLA Ops:
  10.3 78.9 %all-gather.4.cloned.1.call-done = bf16[4,32,128,128]{3,2,1,0:T(8,128)(2,1)} async-done(((bf16[4,4,128,128]{3,2,1,0:T(8,128)(2,1)}), bf16[4,32,128,128]{3,2,1,0:T(8,128)(2,1)}) %all-gather.4.cloned.1.call-update) | async-done | bytes 4194320 | tf_op jit(solution)/shard_map/all_gather | solution.py:97
  89.2 2.9 fusion
  92.1 2.5 fusion.12
  94.6 2.1 reshape_reshape_reshape.6
  96.7 4.2 %copy.31 = f32[2,16,512,32]{2,3,1,0:T(8,128)} copy(f32[2,16,512,32]{2,0,1,3:T(2,128)} %bitcast.126) | data formatting | bytes 4194304 | tf_op jit(solution)/shard_map/transpose | solution.py:20
  101.6 5.4 %all-to-all-start = ((bf16[8,512,32]{1,2,0:T(8,128)(2,1)}), bf16[8,512,32]{1,2,0:T(8,128)(2,1)S(1)}, u32[]{:S(2)}, u32[]{:S(2)}) async-start(bf16[8,512,32]{1,2,0:T(8,128)(2,1)} %broadcast_in_dim.41), calls=%async_computation | async-start | bytes 524288 | tf_op jit(solution)/shard_map/all_to_all | solution.py:33
  107.0 6.1 %all-to-all-done = bf16[8,512,32]{1,2,0:T(8,128)(2,1)S(1)} async-done(((bf16[8,512,32]{1,2,0:T(8,128)(2,1)}), bf16[8,512,32]{1,2,0:T(8,128)(2,1)S(1)}, u32[]{:S(2)}, u32[]{:S(2)}) %all-to-all-start) | async-done | bytes 262176 | tf_op jit(solution)/shard_map/all_to_all | solution.py:33
  115.7 62.1 %all-gather.6.cloned.1.call-done = bf16[16384,32]{0,1:T(8,128)(2,1)} async-done(((bf16[512,32]{0,1:T(8,128)(2,1)}), bf16[16384,32]{0,1:T(8,128)(2,1)}) %all-gather.6.cloned.1.call-update) | async-done | bytes 1048592 | tf_op jit(solution)/shard_map/all_gather | solution.py:60
  180.0 11.1 %reduce-scatter.7.cloned.1.call-done = f32[1,512,32]{1,2,0:T(8,128)} async-done(((f32[16,512,32]{1,2,0:T(8,128)}), f32[1,512,32]{1,2,0:T(8,128)}) %reduce-scatter.7.cloned.1.call-update) | async-done | bytes 65552 | tf_op jit(solution)/shard_map/reduce_scatter | solution.py:22
  191.1 1.8 convolution_bitcast_fusion
  192.9 6.9 %all-to-all-start.2 = ((f32[8,512,32]{1,2,0:T(8,128)}), f32[8,512,32]{1,2,0:T(8,128)S(1)}, u32[]{:S(2)}, u32[]{:S(2)}) async-start(f32[8,512,32]{1,2,0:T(8,128)} %convolution_bitcast_fusion), calls=%async_computation.4 | async-start | bytes 1048576 | tf_op jit(solution)/shard_map/all_to_all | solution.py:49
  199.8 3.3 fusion.3
  203.2 4.2 %all-to-all-done.2 = f32[8,512,32]{1,2,0:T(8,128)S(1)} async-done(((f32[8,512,32]{1,2,0:T(8,128)}), f32[8,512,32]{1,2,0:T(8,128)S(1)}, u32[]{:S(2)}, u32[]{:S(2)}) %all-to-all-start.2) | async-done | bytes 524320 | tf_op jit(solution)/shard_map/all_to_all | solution.py:49
  207.4 2.9 fusion.1
  210.3 2.5 fusion.15
  212.8 2.1 reshape_reshape_reshape.7
  214.9 4.2 %copy.34 = f32[16,2,512,32]{2,3,0,1:T(8,128)} copy(f32[16,2,512,32]{2,1,0,3:T(2,128)} %reshape_reshape_reshape.7) | data formatting | bytes 4194304 | tf_op jit(solution)/shard_map/reshape;reshape;reshape | solution.py:20
  219.2 9.7 %reduce-scatter.9.cloned.1.call-done = f32[16,512,32]{1,2,0:T(8,128)} async-done(((f32[32,512,32]{1,2,0:T(8,128)}), f32[16,512,32]{1,2,0:T(8,128)}) %reduce-scatter.9.cloned.1.call-update) | async-done | bytes 1048592 | tf_op jit(solution)/shard_map/reduce_scatter | solution.py:21
  229.0 13.6 %all_to_all.25 = bf16[8,512,32]{1,2,0:T(8,128)(2,1)S(1)} all-to-all(bf16[8,512,32]{1,2,0:T(8,128)(2,1)S(1)} %broadcast_in_dim.71), channel_id=1, replica_groups=mesh['dom_0'=2,'dom_1'=8,'dom_2'=2,'col'=8] {'col'}, dimensions={0} | all-to-all | bytes 524288 | tf_op jit(solution)/shard_map/all_to_all | solution.py:33
  244.5 7.4 %all-to-all-start.4 = ((bf16[32,256,32]{1,2,0:T(8,128)(2,1)}), bf16[32,256,32]{1,2,0:T(8,128)(2,1)S(1)}, u32[]{:S(2)}, u32[]{:S(2)}) async-start(bf16[32,256,32]{1,2,0:T(8,128)(2,1)} %broadcast_in_dim.73), calls=%async_computation.8 | async-start | bytes 1048576 | tf_op jit(solution)/shard_map/all_to_all | solution.py:33
  251.9 54.8 %reduce-scatter.11.cloned.1.call-done = f32[1,512,32]{1,2,0:T(8,128)} async-done(((f32[16,512,32]{1,2,0:T(8,128)}), f32[1,512,32]{1,2,0:T(8,128)}) %reduce-scatter.11.cloned.1.call-update) | async-done | bytes 65552 | tf_op jit(solution)/shard_map/reduce_scatter | solution.py:22
  308.6 3.9 %all-to-all-start.3 = ((bf16[32,256,32]{1,2,0:T(8,128)(2,1)}), bf16[32,256,32]{1,2,0:T(8,128)(2,1)S(1)}, u32[]{:S(2)}, u32[]{:S(2)}) async-start(bf16[32,256,32]{1,2,0:T(8,128)(2,1)} %broadcast_in_dim.72), calls=%async_computation.7 | async-start | bytes 1048576 | tf_op jit(solution)/shard_map/all_to_all | solution.py:33
  314.7 3.3 fusion.18
  319.4 11.6 %all-to-all-done.3 = bf16[32,256,32]{1,2,0:T(8,128)(2,1)S(1)} async-done(((bf16[32,256,32]{1,2,0:T(8,128)(2,1)}), bf16[32,256,32]{1,2,0:T(8,128)(2,1)S(1)}, u32[]{:S(2)}, u32[]{:S(2)}) %all-to-all-start.3) | async-done | bytes 524320 | tf_op jit(solution)/shard_map/all_to_all | solution.py:33
  (51 shorter events, 16.0 us)
Async XLA Ops:
  8.0 105.2 %copy-start = (bf16[256,256]{1,0:T(8,128)(2,1)S(1)}, bf16[256,256]{1,0:T(8,128)(2,1)}, u32[]{:S(2)}) copy-start(bf16[256,256]{1,0:T(8,128)(2,1)} %param.8) | copy-start | bytes 393220
  8.0 84.1 %copy-start.2 = (s32[4,32]{1,0:T(4,128)S(1)}, s32[4,32]{1,0:T(4,128)}, u32[]{:S(2)}) copy-start(s32[4,32]{1,0:T(4,128)} %param.10) | copy-start | bytes 1540
  8.0 81.1 %all-gather.4.cloned.1.call-start = ((), (), s32[]{:S(2)}) async-start(), calls=%async_computation.9 | async-start | bytes 4718592 | tf_op jit(solution)/shard_map/all_gather | solution.py:97
  8.8 106.7 %reduce-scatter.5.cloned.1.call-start = ((), (), s32[]{:S(2)}) async-start(), calls=%async_computation.12 | async-start | bytes 3145728 | tf_op jit(solution)/shard_map/reduce_scatter | solution.py:21
  96.7 4.2 %copy-start.3 = (bf16[512,32]{0,1:T(8,128)(2,1)S(1)}, bf16[512,32]{0,1:T(8,128)(2,1)}, u32[]{:S(2)}) copy-start(bf16[512,32]{0,1:T(8,128)(2,1)} %param.7) | copy-start | bytes 98308
  96.7 18.9 %copy-start.4 = (bf16[256,256]{1,0:T(8,128)(2,1)S(1)}, bf16[256,256]{1,0:T(8,128)(2,1)}, u32[]{:S(2)}) copy-start(bf16[256,256]{1,0:T(8,128)(2,1)} %param.9) | copy-start | bytes 393220
  101.6 11.5 %all-to-all-start = ((bf16[8,512,32]{1,2,0:T(8,128)(2,1)}), bf16[8,512,32]{1,2,0:T(8,128)(2,1)S(1)}, u32[]{:S(2)}, u32[]{:S(2)}) async-start(bf16[8,512,32]{1,2,0:T(8,128)(2,1)} %broadcast_in_dim.41), calls=%async_computation | async-start | bytes 524288 | tf_op jit(solution)/shard_map/all_to_all | solution.py:33
  107.0 70.8 %all-gather.6.cloned.1.call-start = ((), (), s32[]{:S(2)}) async-start(), calls=%async_computation.10 | async-start | bytes 1081344 | tf_op jit(solution)/shard_map/all_gather | solution.py:60
  114.0 77.0 %reduce-scatter.7.cloned.1.call-start = ((), (), s32[]{:S(2)}) async-start(), calls=%async_computation.13 | async-start | bytes 1114112 | tf_op jit(solution)/shard_map/reduce_scatter | solution.py:22
  192.9 14.4 %all-to-all-start.2 = ((f32[8,512,32]{1,2,0:T(8,128)}), f32[8,512,32]{1,2,0:T(8,128)S(1)}, u32[]{:S(2)}, u32[]{:S(2)}) async-start(f32[8,512,32]{1,2,0:T(8,128)} %convolution_bitcast_fusion), calls=%async_computation.4 | async-start | bytes 1048576 | tf_op jit(solution)/shard_map/all_to_all | solution.py:49
  199.8 29.0 %reduce-scatter.9.cloned.1.call-start = ((), (), s32[]{:S(2)}) async-start(), calls=%async_computation.14 | async-start | bytes 3145728 | tf_op jit(solution)/shard_map/reduce_scatter | solution.py:21
  214.9 28.5 %copy-start.1 = (f32[1,512,32]{1,2,0:T(8,128)S(1)}, f32[1,512,32]{1,2,0:T(8,128)}, u32[]{:S(2)}) copy-start(f32[1,512,32]{1,2,0:T(8,128)} %reduce-scatter.7.cloned.1.call-done) | copy-start | bytes 196612
  219.1 87.5 %reduce-scatter.11.cloned.1.call-start = ((), (), s32[]{:S(2)}) async-start(), calls=%async_computation.15 | async-start | bytes 1114112 | tf_op jit(solution)/shard_map/reduce_scatter | solution.py:22
  228.8 83.7 %all-gather.8.cloned.1.call-start = ((), (), s32[]{:S(2)}) async-start(), calls=%async_computation.11 | async-start | bytes 1081344 | tf_op jit(solution)/shard_map/all_gather | solution.py:60
  244.5 63.2 %all-to-all-start.4 = ((bf16[32,256,32]{1,2,0:T(8,128)(2,1)}), bf16[32,256,32]{1,2,0:T(8,128)(2,1)S(1)}, u32[]{:S(2)}, u32[]{:S(2)}) async-start(bf16[32,256,32]{1,2,0:T(8,128)(2,1)} %broadcast_in_dim.73), calls=%async_computation.8 | async-start | bytes 1048576 | tf_op jit(solution)/shard_map/all_to_all | solution.py:33
  308.6 22.4 %all-to-all-start.3 = ((bf16[32,256,32]{1,2,0:T(8,128)(2,1)}), bf16[32,256,32]{1,2,0:T(8,128)(2,1)S(1)}, u32[]{:S(2)}, u32[]{:S(2)}) async-start(bf16[32,256,32]{1,2,0:T(8,128)(2,1)} %broadcast_in_dim.72), calls=%async_computation.7 | async-start | bytes 1048576 | tf_op jit(solution)/shard_map/all_to_all | solution.py:33
Sparse Core Ops, SparseCore 0:
  11.4 77.6 all-gather.3
  101.0 14.4 reduce-scatter.4
  118.2 72.8 reduce-scatter.6
  219.2 9.5 reduce-scatter.8
  231.3 75.2 reduce-scatter.10
Sparse Core Ops, SparseCore 1:
  114.1 63.6 all-gather.5
  243.5 67.1 all-gather.7
where the time goes:
time: 340 us; the launch traced here: 339 us
  waiting for transfers between devices  241 us (71%)
  starting transfers between devices  23.8 us (7%)
  matrix products  22.1 us (6%)
  local copies, waits for them, and re-layouts  21.1 us (6%)
  between operations  15.4 us (5%)
  blocking collectives  13.6 us (4%)
    all_gather x1, waiting for transfers between devices, body(): all_vals = lax.all_gather(block_vals, 'col', axis=1, tiled=True)  78.9 us
    reduce_scatter x2, waiting for transfers between devices, sum_by_chip(): return lax.psum_scatter(pieces, chips, scatter_dimension=0, tiled=True)[0]  65.8 us
    all_gather x2, waiting for transfers between devices, forward_fold(): piece = lax.all_gather(prod, DOM, axis=0, tiled=True)  62.1 us
    all_to_all x3, waiting for transfers between devices, sent_to_all(): lax.all_to_all(jnp.broadcast_to(shard[None], (peers, *shard.shape)), axis...  17.7 us
    all_to_all x3, starting transfers between devices, sent_to_all(): lax.all_to_all(jnp.broadcast_to(shard[None], (peers, *shard.shape)), axis...  16.7 us
    all_to_all x1, blocking collectives, sent_to_all(): lax.all_to_all(jnp.broadcast_to(shard[None], (peers, *shard.shape)), axis...  13.6 us
    reduce_scatter x2, waiting for transfers between devices, sum_by_chip(): pieces = lax.psum_scatter(pieces, core, scatter_dimension=0, tiled=True)  11.1 us
    another operation x3, local copies, waits for them, and re-layouts, sum_by_chip(): pieces = pieces.reshape(*sizes, *inside).swapaxes(0, 1).reshape(-1, *inside)  8.41 us
  transfers between devices with their start and end apart: 11, of which 9 were waited for; matrix products, arithmetic and copies ran while one was open for 6% of the time, Pallas kernels for 0%

commit v1 on v0

--- a/solution.py
+++ b/solution.py
@@ -94,7 +94,9 @@
             jnp.dot(full.T, back, preferred_element_type=jnp.float32).astype(jnp.bfloat16), DOM
         ).astype(jnp.float32)
 
-    all_vals = lax.all_gather(block_vals, "col", axis=1, tiled=True)
+    all_vals = jnp.concatenate(
+        lax.all_to_all(jnp.stack([block_vals] * lax.axis_size("col")), "col", 0, 0), axis=1
+    )
     slot_ids = jnp.arange(all_vals.shape[1])
     usable = slot_ids[None, :] < block_count[:, None]
     vals = jnp.where(usable[:, :, None, None], all_vals, jnp.zeros((), all_vals.dtype))

time: 340 us -> 322 us (0.947)
  waiting for transfers between devices: 241 us -> 211 us
  local copies, waits for them, and re-layouts: 21.1 us -> 28.9 us
  starting transfers between devices: 23.8 us -> 31 us
    all_gather x1 -> x0, waiting for transfers between devices: 78.9 us -> none  [body(): all_vals = lax.all_gather(block_vals, 'col', axis=1, tiled=True)]
    all_to_all x0 -> x1, waiting for transfers between devices: none -> 48.3 us  [body(): lax.all_to_all(jnp.stack([block_vals] * lax.axis_size('col')), 'col', 0, 0)]
    all_to_all x0 -> x1, starting transfers between devices: none -> 7.39 us  [body(): lax.all_to_all(jnp.stack([block_vals] * lax.axis_size('col')), 'col', 0, 0)]
    another operation x0 -> x1, local copies, waits for them, and re-layouts: none -> 4.1 us  [body(): jnp.stack([block_vals] * lax.axis_size('col'))]
where the time goes in v1:
time: 322 us; the launch traced here: 321 us
  waiting for transfers between devices  211 us (66%)
  starting transfers between devices  31 us (10%)
  local copies, waits for them, and re-layouts  28.9 us (9%)
  matrix products  19.9 us (6%)
  between operations  15.4 us (5%)
  blocking collectives  13.6 us (4%)
    reduce_scatter x2, waiting for transfers between devices, sum_by_chip(): return lax.psum_scatter(pieces, chips, scatter_dimension=0, tiled=True)[0]  65.4 us
    all_gather x2, waiting for transfers between devices, forward_fold(): piece = lax.all_gather(prod, DOM, axis=0, tiled=True)  62.5 us
    all_to_all x1, waiting for transfers between devices, body(): lax.all_to_all(jnp.stack([block_vals] * lax.axis_size('col')), 'col', 0, 0)  48.3 us
    all_to_all x3, waiting for transfers between devices, sent_to_all(): lax.all_to_all(jnp.broadcast_to(shard[None], (peers, *shard.shape)), axis...  17.9 us
    all_to_all x3, starting transfers between devices, sent_to_all(): lax.all_to_all(jnp.broadcast_to(shard[None], (peers, *shard.shape)), axis...  16.6 us
    all_to_all x1, blocking collectives, sent_to_all(): lax.all_to_all(jnp.broadcast_to(shard[None], (peers, *shard.shape)), axis...  13.6 us
    reduce_scatter x2, waiting for transfers between devices, sum_by_chip(): pieces = lax.psum_scatter(pieces, core, scatter_dimension=0, tiled=True)  12.3 us
    another operation x3, local copies, waits for them, and re-layouts, sum_by_chip(): pieces = pieces.reshape(*sizes, *inside).swapaxes(0, 1).reshape(-1, *inside)  8.44 us
  transfers between devices with their start and end apart: 11, of which 9 were waited for; matrix products, arithmetic and copies ran while one was open for 6% of the time, Pallas kernels for 0%

profile of v1, /device:TPU:16, one launch (start us, length us, event | category | flops | bytes accessed | tf_op | source)
XLA Modules:
  0.0 321.1 jit_solution(9803923062320833605)
XLA Ops:
  8.0 4.1 %stack.2 = bf16[8,4,4,128,128]{4,3,2,1,0:T(8,128)(2,1)} broadcast(bf16[4,4,128,128]{3,2,1,0:T(8,128)(2,1)} %param.12), dimensions={1,2,3,4} | broadcast | bytes 4718592 | tf_op jit(solution)/shard_map/stack | solution.py:98
  12.1 7.4 %all-to-all-start = ((bf16[8,4,4,128,128]{4,3,2,1,0:T(8,128)(2,1)}), bf16[8,4,4,128,128]{4,3,2,1,0:T(8,128)(2,1)}, u32[]{:S(2)}, u32[]{:S(2)}) async-start(bf16[8,4,4,128,128]{4,3,2,1,0:T(8,128)(2,1)} %stack.2), calls=%async_computation | async-start | bytes 8388608 | tf_op jit(solution)/shard_map/all_to_all | solution.py:98
  19.6 48.3 %all-to-all-done = bf16[8,4,4,128,128]{4,3,2,1,0:T(8,128)(2,1)} async-done(((bf16[8,4,4,128,128]{4,3,2,1,0:T(8,128)(2,1)}), bf16[8,4,4,128,128]{4,3,2,1,0:T(8,128)(2,1)}, u32[]{:S(2)}, u32[]{:S(2)}) %all-to-all-start) | async-done | bytes 4194336 | tf_op jit(solution)/shard_map/all_to_all | solution.py:98
  67.9 2.5 copy.35
  73.2 2.5 fusion.12
  77.7 4.2 %copy.42 = f32[2,16,512,32]{2,3,1,0:T(8,128)} copy(f32[2,16,512,32]{2,0,1,3:T(2,128)} %bitcast.133) | data formatting | bytes 4194304 | tf_op jit(solution)/shard_map/transpose | solution.py:20
  82.7 5.3 %all-to-all-start.1 = ((bf16[8,512,32]{1,2,0:T(8,128)(2,1)}), bf16[8,512,32]{1,2,0:T(8,128)(2,1)S(1)}, u32[]{:S(2)}, u32[]{:S(2)}) async-start(bf16[8,512,32]{1,2,0:T(8,128)(2,1)} %broadcast_in_dim.41), calls=%async_computation.1 | async-start | bytes 524288 | tf_op jit(solution)/shard_map/all_to_all | solution.py:33
  88.0 6.3 %all-to-all-done.1 = bf16[8,512,32]{1,2,0:T(8,128)(2,1)S(1)} async-done(((bf16[8,512,32]{1,2,0:T(8,128)(2,1)}), bf16[8,512,32]{1,2,0:T(8,128)(2,1)S(1)}, u32[]{:S(2)}, u32[]{:S(2)}) %all-to-all-start.1) | async-done | bytes 262176 | tf_op jit(solution)/shard_map/all_to_all | solution.py:33
  95.2 2.7 reduce-scatter.5.cloned.1.call-done
  98.2 62.5 %all-gather.3.cloned.1.call-done = bf16[16384,32]{0,1:T(8,128)(2,1)} async-done(((bf16[512,32]{0,1:T(8,128)(2,1)}), bf16[16384,32]{0,1:T(8,128)(2,1)}) %all-gather.3.cloned.1.call-update) | async-done | bytes 1048592 | tf_op jit(solution)/shard_map/all_gather | solution.py:60
  162.8 10.6 %reduce-scatter.7.cloned.1.call-done = f32[1,512,32]{1,2,0:T(8,128)} async-done(((f32[16,512,32]{1,2,0:T(8,128)}), f32[1,512,32]{1,2,0:T(8,128)}) %reduce-scatter.7.cloned.1.call-update) | async-done | bytes 65552 | tf_op jit(solution)/shard_map/reduce_scatter | solution.py:22
  175.3 6.9 %all-to-all-start.3 = ((f32[8,512,32]{1,2,0:T(8,128)}), f32[8,512,32]{1,2,0:T(8,128)S(1)}, u32[]{:S(2)}, u32[]{:S(2)}) async-start(f32[8,512,32]{1,2,0:T(8,128)} %convolution_bitcast_fusion), calls=%async_computation.5 | async-start | bytes 1048576 | tf_op jit(solution)/shard_map/all_to_all | solution.py:49
  182.2 3.3 %fusion.3 = f32[4,128,32,1]{1,2,3,0:T(8,128)S(1)} fusion(bf16[4,32,128,128]{3,2,1,0:T(8,128)(2,1)} %bitcast.126, pred[4,32]{1,0:T(4,128)(4,1)S(1)} %iota_compare_fusion.1, bf16[4,32,128,32]{2,3,1,0:T(8,128)(2,1)S(1)} %bitcast.129, pred[4,32]{1,0:T(4,128)(4,1)S(1)} %compare_and_fusion), kind=kOutput, calls=%fused_computation.6 | convolution fusion | flops 136839168 | bytes 5308672 | tf_op jit(solution)/shard_map/rkij,rkjf->rif/dot_general | solution.py:65
  185.6 4.2 %all-to-all-done.3 = f32[8,512,32]{1,2,0:T(8,128)S(1)} async-done(((f32[8,512,32]{1,2,0:T(8,128)}), f32[8,512,32]{1,2,0:T(8,128)S(1)}, u32[]{:S(2)}, u32[]{:S(2)}) %all-to-all-start.3) | async-done | bytes 524320 | tf_op jit(solution)/shard_map/all_to_all | solution.py:49
  189.8 2.9 fusion.1
  192.7 2.5 fusion.15
  197.3 4.2 %copy.45 = f32[16,2,512,32]{2,3,0,1:T(8,128)} copy(f32[16,2,512,32]{2,1,0,3:T(2,128)} %reshape_reshape_reshape.7) | data formatting | bytes 4194304 | tf_op jit(solution)/shard_map/reshape;reshape;reshape | solution.py:20
  201.6 9.6 %reduce-scatter.9.cloned.1.call-done = f32[16,512,32]{1,2,0:T(8,128)} async-done(((f32[32,512,32]{1,2,0:T(8,128)}), f32[16,512,32]{1,2,0:T(8,128)}) %reduce-scatter.9.cloned.1.call-update) | async-done | bytes 1048592 | tf_op jit(solution)/shard_map/reduce_scatter | solution.py:21
  211.3 13.6 %all_to_all.30 = bf16[8,512,32]{1,2,0:T(8,128)(2,1)S(1)} all-to-all(bf16[8,512,32]{1,2,0:T(8,128)(2,1)S(1)} %broadcast_in_dim.71), channel_id=1, replica_groups=mesh['dom_0'=2,'dom_1'=8,'dom_2'=2,'col'=8] {'col'}, dimensions={0} | all-to-all | bytes 524288 | tf_op jit(solution)/shard_map/all_to_all | solution.py:33
  226.8 7.4 %all-to-all-start.5 = ((bf16[32,256,32]{1,2,0:T(8,128)(2,1)}), bf16[32,256,32]{1,2,0:T(8,128)(2,1)S(1)}, u32[]{:S(2)}, u32[]{:S(2)}) async-start(bf16[32,256,32]{1,2,0:T(8,128)(2,1)} %broadcast_in_dim.73), calls=%async_computation.9 | async-start | bytes 1048576 | tf_op jit(solution)/shard_map/all_to_all | solution.py:33
  234.2 54.8 %reduce-scatter.11.cloned.1.call-done = f32[1,512,32]{1,2,0:T(8,128)} async-done(((f32[16,512,32]{1,2,0:T(8,128)}), f32[1,512,32]{1,2,0:T(8,128)}) %reduce-scatter.11.cloned.1.call-update) | async-done | bytes 65552 | tf_op jit(solution)/shard_map/reduce_scatter | solution.py:22
  291.0 3.9 %all-to-all-start.4 = ((bf16[32,256,32]{1,2,0:T(8,128)(2,1)}), bf16[32,256,32]{1,2,0:T(8,128)(2,1)S(1)}, u32[]{:S(2)}, u32[]{:S(2)}) async-start(bf16[32,256,32]{1,2,0:T(8,128)(2,1)} %broadcast_in_dim.72), calls=%async_computation.8 | async-start | bytes 1048576 | tf_op jit(solution)/shard_map/all_to_all | solution.py:33
  297.1 3.3 %fusion.18 = f32[4,4,8,128]{3,2,1,0:T(8,128)S(1)} fusion(bf16[4,32,128,128]{3,2,1,0:T(8,128)(2,1)} %bitcast.128, pred[4,32]{1,0:T(4,128)(4,1)S(1)} %iota_compare_fusion.1, bf16[4,32,128,32]{2,3,1,0:T(8,128)(2,1)S(1)} %bitcast.130, pred[4,32]{1,0:T(4,128)(4,1)S(1)} %compare_and_fusion), kind=kOutput, calls=%fused_computation.18 | convolution fusion | flops 136839168 | bytes 5308672 | tf_op jit(solution)/shard_map/rkij,rkjf->rif/dot_general | solution.py:65
  301.7 11.6 %all-to-all-done.4 = bf16[32,256,32]{1,2,0:T(8,128)(2,1)S(1)} async-done(((bf16[32,256,32]{1,2,0:T(8,128)(2,1)}), bf16[32,256,32]{1,2,0:T(8,128)(2,1)S(1)}, u32[]{:S(2)}, u32[]{:S(2)}) %all-to-all-start.4) | async-done | bytes 524320 | tf_op jit(solution)/shard_map/all_to_all | solution.py:33
  (58 shorter events, 21.2 us)
Async XLA Ops:
  8.0 86.3 %copy-start = (bf16[256,256]{1,0:T(8,128)(2,1)S(1)}, bf16[256,256]{1,0:T(8,128)(2,1)}, u32[]{:S(2)}) copy-start(bf16[256,256]{1,0:T(8,128)(2,1)} %param.8) | copy-start | bytes 393220
  12.1 7.4 %copy-start.6 = (bf16[512,32]{0,1:T(8,128)(2,1)S(1)}, bf16[512,32]{0,1:T(8,128)(2,1)}, u32[]{:S(2)}) copy-start(bf16[512,32]{0,1:T(8,128)(2,1)} %param.13) | copy-start | bytes 98308
  12.1 7.4 %copy-start.7 = (s32[4]{0:T(128)S(1)}, s32[4]{0:T(128)}, u32[]{:S(2)}) copy-start(s32[4]{0:T(128)} %param.11) | copy-start | bytes 52
  12.1 55.8 %all-to-all-start = ((bf16[8,4,4,128,128]{4,3,2,1,0:T(8,128)(2,1)}), bf16[8,4,4,128,128]{4,3,2,1,0:T(8,128)(2,1)}, u32[]{:S(2)}, u32[]{:S(2)}) async-start(bf16[8,4,4,128,128]{4,3,2,1,0:T(8,128)(2,1)} %stack.2), calls=%async_computation | async-start | bytes 8388608 | tf_op jit(solution)/shard_map/all_to_all | solution.py:98
  19.5 78.4 %reduce-scatter.5.cloned.1.call-start = ((), (), s32[]{:S(2)}) async-start(), calls=%async_computation.12 | async-start | bytes 3145728 | tf_op jit(solution)/shard_map/reduce_scatter | solution.py:21
  70.4 2.0 copy-start.1
  70.5 2.7 copy-start.3
  77.7 4.2 %copy-start.4 = (bf16[512,32]{0,1:T(8,128)(2,1)S(1)}, bf16[512,32]{0,1:T(8,128)(2,1)}, u32[]{:S(2)}) copy-start(bf16[512,32]{0,1:T(8,128)(2,1)} %param.7) | copy-start | bytes 98308
  77.7 20.3 %copy-start.5 = (bf16[256,256]{1,0:T(8,128)(2,1)S(1)}, bf16[256,256]{1,0:T(8,128)(2,1)}, u32[]{:S(2)}) copy-start(bf16[256,256]{1,0:T(8,128)(2,1)} %param.9) | copy-start | bytes 393220
  82.7 11.6 %all-to-all-start.1 = ((bf16[8,512,32]{1,2,0:T(8,128)(2,1)}), bf16[8,512,32]{1,2,0:T(8,128)(2,1)S(1)}, u32[]{:S(2)}, u32[]{:S(2)}) async-start(bf16[8,512,32]{1,2,0:T(8,128)(2,1)} %broadcast_in_dim.41), calls=%async_computation.1 | async-start | bytes 524288 | tf_op jit(solution)/shard_map/all_to_all | solution.py:33
  88.0 72.6 %all-gather.3.cloned.1.call-start = ((), (), s32[]{:S(2)}) async-start(), calls=%async_computation.10 | async-start | bytes 1081344 | tf_op jit(solution)/shard_map/all_gather | solution.py:60
  95.2 78.3 %reduce-scatter.7.cloned.1.call-start = ((), (), s32[]{:S(2)}) async-start(), calls=%async_computation.13 | async-start | bytes 1114112 | tf_op jit(solution)/shard_map/reduce_scatter | solution.py:22
  175.3 14.4 %all-to-all-start.3 = ((f32[8,512,32]{1,2,0:T(8,128)}), f32[8,512,32]{1,2,0:T(8,128)S(1)}, u32[]{:S(2)}, u32[]{:S(2)}) async-start(f32[8,512,32]{1,2,0:T(8,128)} %convolution_bitcast_fusion), calls=%async_computation.5 | async-start | bytes 1048576 | tf_op jit(solution)/shard_map/all_to_all | solution.py:49
  182.2 29.0 %reduce-scatter.9.cloned.1.call-start = ((), (), s32[]{:S(2)}) async-start(), calls=%async_computation.14 | async-start | bytes 3145728 | tf_op jit(solution)/shard_map/reduce_scatter | solution.py:21
  197.3 28.4 %copy-start.2 = (f32[1,512,32]{1,2,0:T(8,128)S(1)}, f32[1,512,32]{1,2,0:T(8,128)}, u32[]{:S(2)}) copy-start(f32[1,512,32]{1,2,0:T(8,128)} %reduce-scatter.7.cloned.1.call-done) | copy-start | bytes 196612
  201.5 87.5 %reduce-scatter.11.cloned.1.call-start = ((), (), s32[]{:S(2)}) async-start(), calls=%async_computation.15 | async-start | bytes 1114112 | tf_op jit(solution)/shard_map/reduce_scatter | solution.py:22
  211.2 83.7 %all-gather.5.cloned.1.call-start = ((), (), s32[]{:S(2)}) async-start(), calls=%async_computation.11 | async-start | bytes 1081344 | tf_op jit(solution)/shard_map/all_gather | solution.py:60
  226.8 63.2 %all-to-all-start.5 = ((bf16[32,256,32]{1,2,0:T(8,128)(2,1)}), bf16[32,256,32]{1,2,0:T(8,128)(2,1)S(1)}, u32[]{:S(2)}, u32[]{:S(2)}) async-start(bf16[32,256,32]{1,2,0:T(8,128)(2,1)} %broadcast_in_dim.73), calls=%async_computation.9 | async-start | bytes 1048576 | tf_op jit(solution)/shard_map/all_to_all | solution.py:33
  291.0 22.4 %all-to-all-start.4 = ((bf16[32,256,32]{1,2,0:T(8,128)(2,1)}), bf16[32,256,32]{1,2,0:T(8,128)(2,1)S(1)}, u32[]{:S(2)}, u32[]{:S(2)}) async-start(bf16[32,256,32]{1,2,0:T(8,128)(2,1)} %broadcast_in_dim.72), calls=%async_computation.8 | async-start | bytes 1048576 | tf_op jit(solution)/shard_map/all_to_all | solution.py:33
Sparse Core Ops, SparseCore 0:
  82.1 15.7 reduce-scatter.4
  100.6 72.8 reduce-scatter.6
  201.6 9.4 reduce-scatter.8
  213.7 75.2 reduce-scatter.10
Sparse Core Ops, SparseCore 1:
  95.3 65.3 all-gather.2
  225.8 67.0 all-gather.4
